TPU v7x, 128 devices: a whole 4x4x4 slice. The times are simulated.
128 devices in a mesh: tile: 64 (over z, x, y), mode: 2 (over core).
Axes of the slice: x: 4, y: 4, z: 4, core: 2. Of those that a mesh axis runs over, the one named last changes fastest.
Arguments:
- obj: float32 [64, 2, 384, 384], P('tile'), may hold values from -6 to 6
- probe: float32 [4, 2, 256, 256], P('mode'), may hold values from -3 to 3
- mode_weights: float32 [8, 4], P(None, 'mode'), may hold values from 0.25 to 1
- measured: float32 [256, 256, 256], P('tile'), may hold values from 0 to 4
- corner: int32 [256, 2], P('tile'), may hold values from 0 to 383, as said below
- counts: int32 [64], P('tile'), may hold values from 1 to 4, 128 in all
- weight_index: int32 [256], P('tile'), may hold values from 0 to 7
Outputs:
- obj_new: float32 [64, 2, 384, 384], P('tile')
- probe_new: float32 [4, 2, 256, 256], P('mode')
Inputs may be any that keep to these rules, and one draw needn't show every extreme that they name: Tile t has live slots 0 to counts[t] - 1 of its block; the counts sum to 128 and some tile has 4. The first slot of every tile has both corner coordinates between 192 and 320.
All inputs are finite; a program needn't handle non-finite values.
Results may differ from a plain program's by a relative error of at most 0.019.
The roundings to bfloat16 on the way count: a program that leaves them out, or rounds other values in their place, can miss the bound.
Values may be sent and summed in bfloat16 or wider, within the bound.
A program may use at most 64 MiB of HBM per device.

v0:
```python
import math

import jax
import jax.numpy as jnp
from jax import lax
from jax.sharding import PartitionSpec as P

GC = 8
POS_DEV = 2
ITERS = 2


step_object = 0.1
step_probe = 4.0


def shifted(array, axis, by):
    peers = lax.axis_size(axis)
    return lax.ppermute(array, axis, [(i, (i + by) % peers) for i in range(peers)])


def dft_tables(length, sign):
    index = jnp.arange(length, dtype=jnp.int32)
    product = index[:, None] * index[None, :] % length
    angle = product.astype(jnp.float32) * (2.0 * math.pi / length)
    factor = 1.0 / math.sqrt(length)
    real = jnp.cos(angle) * factor
    imag = sign * jnp.sin(angle) * factor
    left = jnp.concatenate(
        [jnp.concatenate([real, -imag], 1), jnp.concatenate([imag, real], 1)], 0
    ).astype(jnp.bfloat16)
    right = jnp.concatenate([real, imag], 1).astype(jnp.bfloat16)
    return (left, right)


def transform(field, tables):
    left, right = tables
    count = field.shape[0]
    length = field.shape[-1]
    first = jnp.einsum(
        "ij,bjk->bik",
        left,
        field.reshape(count, 2 * length, length),
        preferred_element_type=jnp.float32,
    )
    first = first.astype(jnp.bfloat16).reshape(count, 2, length, length)
    second = jnp.einsum("bcjk,kl->bcjl", first, right, preferred_element_type=jnp.float32)
    real = second[:, 0, :, :length] - second[:, 1, :, length:]
    imag = second[:, 0, :, length:] + second[:, 1, :, :length]
    return jnp.stack([real, imag], 1)


def patch_contributions(
    object_patches, measured, active_mask, mode_weighting, probe, forward_pass, backward_pass, total
):
    count = object_patches.shape[0]
    modes = probe.shape[0]
    length = probe.shape[-1]
    obj_part = object_patches.astype(jnp.float32)[:, None]
    probe_part = probe[None]
    exit_real = probe_part[:, :, 0] * obj_part[:, :, 0] - probe_part[:, :, 1] * obj_part[:, :, 1]
    exit_imag = probe_part[:, :, 0] * obj_part[:, :, 1] + probe_part[:, :, 1] * obj_part[:, :, 0]
    exit_wave = jnp.stack([exit_real, exit_imag], 2).astype(jnp.bfloat16)
    psi = transform(exit_wave.reshape(count * modes, 2, length, length), forward_pass).reshape(
        count, modes, 2, length, length
    )
    power = psi[:, :, 0] * psi[:, :, 0] + psi[:, :, 1] * psi[:, :, 1]
    intensity = total(jnp.sum(mode_weighting[:, :, None, None] * power, 1))
    resid = (intensity - measured) * active_mask[:, None, None]
    scaled = (mode_weighting[:, :, None, None, None] * resid[:, None, None] * psi).astype(
        jnp.bfloat16
    )
    chi = transform(scaled.reshape(count * modes, 2, length, length), backward_pass).reshape(
        count, modes, 2, length, length
    )
    obj_real = jnp.sum(probe_part[:, :, 0] * chi[:, :, 0] + probe_part[:, :, 1] * chi[:, :, 1], 1)
    obj_imag = jnp.sum(probe_part[:, :, 0] * chi[:, :, 1] - probe_part[:, :, 1] * chi[:, :, 0], 1)
    probe_real = jnp.sum(obj_part[:, :, 0] * chi[:, :, 0] + obj_part[:, :, 1] * chi[:, :, 1], 0)
    probe_imag = jnp.sum(obj_part[:, :, 0] * chi[:, :, 1] - obj_part[:, :, 1] * chi[:, :, 0], 0)
    return (jnp.stack([obj_real, obj_imag], 1), jnp.stack([probe_real, probe_imag], 1))


def body(obj, probe, mode_weights, measured, corner, counts, weight_index):
    patch = probe.shape[-1]
    tile = obj.shape[-1]
    capacity = measured.shape[0]
    kinds = mode_weights.shape[0]
    zero_index = jnp.zeros((), jnp.int32)
    forward_pass = dft_tables(patch, -1.0)
    backward_pass = dft_tables(patch, 1.0)
    active_mask = (jnp.arange(capacity, dtype=jnp.int32) < counts[0]).astype(jnp.float32)
    onehot = (weight_index[:, None] == jnp.arange(kinds, dtype=jnp.int32)[None, :]).astype(
        jnp.float32
    )
    positions = POS_DEV * lax.axis_size("tile")
    state = obj[0]
    probe_now = probe
    for sweep in range(ITERS):
        half = state.astype(jnp.bfloat16)
        right = shifted(half[:, :, :patch], "tile", -1)
        wide = jnp.concatenate([half, right], 2)
        below = shifted(half[:, :patch, :], "tile", -GC)
        diagonal = shifted(half[:, :patch, :patch], "tile", -(GC + 1))
        lower = jnp.concatenate([below, diagonal], 2)
        padded = jnp.concatenate([wide, lower], 1)

        def cut(spot):
            return lax.dynamic_slice(padded, (zero_index, spot[0], spot[1]), (2, patch, patch))

        object_patches = jax.vmap(cut)(corner)
        mode_weighting = jnp.dot(onehot, mode_weights, precision=lax.Precision.HIGHEST)

        def mode_total(part):
            return lax.psum(part.astype(jnp.bfloat16), "mode").astype(jnp.float32)

        object_terms, probe_updates = patch_contributions(
            object_patches,
            measured,
            active_mask,
            mode_weighting,
            probe_now,
            forward_pass,
            backward_pass,
            mode_total,
        )

        def place(slot, acc):
            spot = corner[slot]
            where = (zero_index, spot[0], spot[1])
            current = lax.dynamic_slice(acc, where, (2, patch, patch))
            return lax.dynamic_update_slice(acc, current + object_terms[slot], where)

        gradient = jnp.zeros((2, tile + patch, tile + patch), jnp.float32)
        gradient = lax.fori_loop(0, object_terms.shape[0], place, gradient)
        above = shifted(gradient[:, tile:, :tile].astype(jnp.bfloat16), "tile", GC).astype(
            jnp.float32
        )
        upper_left = shifted(gradient[:, tile:, tile:].astype(jnp.bfloat16), "tile", GC + 1).astype(
            jnp.float32
        )
        gradient = gradient.at[:, :patch, :tile].add(above)
        gradient = gradient.at[:, :patch, :patch].add(upper_left)
        from_left = shifted(gradient[:, :tile, tile:].astype(jnp.bfloat16), "tile", 1).astype(
            jnp.float32
        )
        tile_grad = gradient[:, :tile, :tile].at[:, :, :patch].add(from_left)
        tile_grad = lax.psum(tile_grad.astype(jnp.bfloat16), "mode").astype(jnp.float32)
        probe_grad = lax.psum(probe_updates, "tile")
        state = state - step_object * tile_grad
        probe_now = probe_now - step_probe / positions * probe_grad
    return (state[None], probe_now)


def solution(mesh):
    placed = (
        P("tile", None, None, None),
        P("mode", None, None, None),
        P(None, "mode"),
        P("tile", None, None),
        P("tile", None),
        P("tile"),
        P("tile"),
    )
    return jax.shard_map(
        body,
        mesh=mesh,
        in_specs=placed,
        out_specs=(P("tile", None, None, None), P("mode", None, None, None)),
        check_vma=False,
    )
```

profile of v0, /device:TPU:1, one launch (start us, length us, event | category | flops | bytes accessed | tf_op | source)
XLA Modules:
  0.0 721.9 jit_solution(17443774101212672292)
XLA Ops:
  9.4 9.2 %collective-permute-start = (bf16[2,384,256]{2,1,0:T(8,128)(2,1)}, bf16[2,384,256]{2,1,0:T(8,128)(2,1)S(1)}, u32[]{:S(2)}, u32[]{:S(2)}) collective-permute-start(bf16[2,384,256]{2,1,0:T(8,128)(2,1)} %slice.449), channel_id=1, source_target_pairs={{0,126},{2,0},{4,2},{6,4},{8,6},{10,8},{12,10},{14,12},{16,14},{18... | collective-permute-start | bytes 1179656 | tf_op jit(solution)/shard_map/ppermute | solution.py:19
  26.4 7.0 collective-permute-done.2
  37.4 8.4 %while.36 = (s32[]{:T(128)}, bf16[2,640,640]{2,1,0:T(8,128)(2,1)S(1)}, s32[4,3]{1,0:T(4,128)S(1)}, bf16[4,2,256,256]{3,2,1,0:T(8,128)(2,1)S(1)}, s32[]{:T(128)}) while((s32[]{:T(128)}, bf16[2,640,640]{2,1,0:T(8,128)(2,1)S(1)}, s32[4,3]{1,0:T(4,128)S(1)}, bf16[4,2,256,256]{3,2,1,0:T(8,128)(2,1)S(1)}, s32[]{:T(128)}) %tuple.139), condition=%wide.while_cond.6, body=%wide.while_body.6.sunk | while | flops 2 | bytes 524405 | solution.py:108
  47.8 6.6 subtract_convert_fusion.1
  75.4 29.2 %all-reduce.7.cloned.1.call-done = bf16[4,256,256]{2,1,0:T(8,128)(2,1)} async-done(((bf16[4,256,256]{2,1,0:T(8,128)(2,1)}), bf16[4,256,256]{2,1,0:T(8,128)(2,1)}) %all-reduce.7.cloned.1.call-update) | async-done | bytes 524304 | tf_op jit(solution)/shard_map/psum | solution.py:114
  109.8 4.9 copy.17
  131.2 50.1 %while.34 = (s32[]{:T(128)}, f32[2,640,640]{2,1,0:T(8,128)}, s32[4,2]{0,1:T(2,128)S(1)}, f32[4,2,256,256]{3,2,1,0:T(8,128)S(1)}, s32[]{:T(128)}, /*index=5*/s32[]{:T(128)}, s32[]{:T(128)}) while((s32[]{:T(128)}, f32[2,640,640]{2,1,0:T(8,128)}, s32[4,2]{0,1:T(2,128)S(1)}, f32[4,2,256,256]{3,2,1,0:T(8,128)S(1)}, s32[]{:T(128)}, ...), condition=%wide.region_5.6_spmd, body=%wide.region_4.5_spmd.sunk | while | flops 131080 | bytes 2621637 | solution.py:134
  137.2 6.7 dynamic_update_slice.16
  150.0 6.5 dynamic_update_slice.16
  162.5 6.8 dynamic_update_slice.16
  175.4 5.9 dynamic_update_slice.16
  188.9 9.8 %collective-permute-done.3 = bf16[2,256,384]{2,1,0:T(8,128)(2,1)S(1)} collective-permute-done((bf16[2,256,384]{2,1,0:T(8,128)(2,1)S(1)}, bf16[2,256,384]{2,1,0:T(8,128)(2,1)S(1)}, u32[]{:S(2)}, u32[]{:S(2)}) %collective-permute-start.3) | collective-permute-done | bytes 393248 | tf_op jit(solution)/shard_map/ppermute | solution.py:19
  199.0 7.2 %collective-permute-done.4 = bf16[2,256,256]{2,1,0:T(8,128)(2,1)S(1)} collective-permute-done((bf16[2,256,256]{2,1,0:T(8,128)(2,1)S(1)}, bf16[2,256,256]{2,1,0:T(8,128)(2,1)S(1)}, u32[]{:S(2)}, u32[]{:S(2)}) %collective-permute-start.4) | collective-permute-done | bytes 262176 | tf_op jit(solution)/shard_map/ppermute | solution.py:19
  206.5 14.9 %collective-permute-done.5 = bf16[2,384,256]{2,1,0:T(8,128)(2,1)S(1)} collective-permute-done((bf16[2,384,256]{2,1,0:T(8,128)(2,1)S(1)}, bf16[2,384,256]{2,1,0:T(8,128)(2,1)S(1)}, u32[]{:S(2)}, u32[]{:S(2)}) %collective-permute-start.5) | collective-permute-done | bytes 393248 | tf_op jit(solution)/shard_map/ppermute | solution.py:19
  223.6 18.7 %all-reduce.9.cloned.1.call-done = bf16[2,384,384]{2,1,0:T(8,128)(2,1)} async-done(((bf16[2,384,384]{2,1,0:T(8,128)(2,1)}), bf16[2,384,384]{2,1,0:T(8,128)(2,1)}) %all-reduce.9.cloned.1.call-update) | async-done | bytes 589840 | tf_op jit(solution)/shard_map/psum | solution.py:147
  245.1 7.1 collective-permute-start.6
  252.7 130.4 %all-reduce.11.cloned.1.call-done = f32[2,2,256,256]{3,2,1,0:T(8,128)} async-done(((f32[2,2,256,256]{3,2,1,0:T(8,128)}), f32[2,2,256,256]{3,2,1,0:T(8,128)}) %all-reduce.11.cloned.1.call-update) | async-done | bytes 1048592 | tf_op jit(solution)/shard_map/psum | solution.py:148
  396.4 11.6 %while.37 = (s32[]{:T(128)}, bf16[2,640,640]{2,1,0:T(8,128)(2,1)S(1)}, s32[4,3]{1,0:T(4,128)S(1)}, bf16[4,2,256,256]{3,2,1,0:T(8,128)(2,1)}, s32[]{:T(128)}) while((s32[]{:T(128)}, bf16[2,640,640]{2,1,0:T(8,128)(2,1)S(1)}, s32[4,3]{1,0:T(4,128)S(1)}, bf16[4,2,256,256]{3,2,1,0:T(8,128)(2,1)}, s32[]{:T(128)}) %tuple.165), condition=%wide.while_cond.7, body=%wide.while_body.7.sunk | while | flops 2 | bytes 525929 | solution.py:108
  411.2 6.6 subtract_convert_fusion
  417.7 4.8 pad_maximum_fusion.2
  437.2 27.1 %all-reduce.13.cloned.1.call-done = bf16[4,256,256]{2,1,0:T(8,128)(2,1)} async-done(((bf16[4,256,256]{2,1,0:T(8,128)(2,1)}), bf16[4,256,256]{2,1,0:T(8,128)(2,1)}) %all-reduce.13.cloned.1.call-update) | async-done | bytes 524304 | tf_op jit(solution)/shard_map/psum | solution.py:114
  469.4 4.9 copy.24
  490.9 48.7 %while.35 = (s32[]{:T(128)}, f32[2,640,640]{2,1,0:T(8,128)}, s32[4,2]{0,1:T(2,128)S(1)}, f32[4,2,256,256]{3,2,1,0:T(8,128)S(1)}, s32[]{:T(128)}, /*index=5*/s32[]{:T(128)}, s32[]{:T(128)}) while((s32[]{:T(128)}, f32[2,640,640]{2,1,0:T(8,128)}, s32[4,2]{0,1:T(2,128)S(1)}, f32[4,2,256,256]{3,2,1,0:T(8,128)S(1)}, s32[]{:T(128)}, ...), condition=%wide.region_15.16_spmd, body=%wide.region_14.15_spmd.sunk | while | flops 131080 | bytes 2621637 | solution.py:134
  496.6 6.7 dynamic_update_slice.17
  509.0 6.5 dynamic_update_slice.17
  521.2 6.8 dynamic_update_slice.17
  533.7 5.9 dynamic_update_slice.17
  549.0 9.0 %collective-permute-done.9 = bf16[2,256,384]{2,1,0:T(8,128)(2,1)} collective-permute-done((bf16[2,256,384]{2,1,0:T(8,128)(2,1)}, bf16[2,256,384]{2,1,0:T(8,128)(2,1)}, u32[]{:S(2)}, u32[]{:S(2)}) %collective-permute-start.9) | collective-permute-done | bytes 393248 | tf_op jit(solution)/shard_map/ppermute | solution.py:19
  559.3 7.1 collective-permute-done.10
  567.5 14.5 %collective-permute-done.11 = bf16[2,384,256]{2,1,0:T(8,128)(2,1)S(1)} collective-permute-done((bf16[2,384,256]{2,1,0:T(8,128)(2,1)S(1)}, bf16[2,384,256]{2,1,0:T(8,128)(2,1)S(1)}, u32[]{:S(2)}, u32[]{:S(2)}) %collective-permute-start.11) | collective-permute-done | bytes 393248 | tf_op jit(solution)/shard_map/ppermute | solution.py:19
  582.9 102.0 %all-reduce.17.cloned.1.call-done = f32[2,2,256,256]{3,2,1,0:T(8,128)} async-done(((f32[2,2,256,256]{3,2,1,0:T(8,128)}), f32[2,2,256,256]{3,2,1,0:T(8,128)}) %all-reduce.17.cloned.1.call-update) | async-done | bytes 1048592 | tf_op jit(solution)/shard_map/psum | solution.py:148
  687.9 24.3 %all-reduce.15.cloned.1.call-done = bf16[2,384,384]{2,1,0:T(8,128)(2,1)} async-done(((bf16[2,384,384]{2,1,0:T(8,128)(2,1)}), bf16[2,384,384]{2,1,0:T(8,128)(2,1)}) %all-reduce.15.cloned.1.call-update) | async-done | bytes 589840 | tf_op jit(solution)/shard_map/psum | solution.py:147
  (250 shorter events, 178.0 us)
Async XLA Ops:
  7.2 19.1 %copy-start = (f32[8,2]{0,1:T(2,128)S(1)}, f32[8,2]{0,1:T(2,128)}, u32[]{:S(2)}) copy-start(f32[8,2]{0,1:T(2,128)} %param.25) | copy-start | bytes 196
  7.2 97.5 %all-reduce.7.cloned.1.call-start = ((), (), s32[]{:S(2)}) async-start(), calls=%async_computation | async-start | bytes 1048576 | tf_op jit(solution)/shard_map/psum | solution.py:114
  9.4 26.6 %collective-permute-start = (bf16[2,384,256]{2,1,0:T(8,128)(2,1)}, bf16[2,384,256]{2,1,0:T(8,128)(2,1)S(1)}, u32[]{:S(2)}, u32[]{:S(2)}) collective-permute-start(bf16[2,384,256]{2,1,0:T(8,128)(2,1)} %slice.449), channel_id=1, source_target_pairs={{0,126},{2,0},{4,2},{6,4},{8,6},{10,8},{12,10},{14,12},{16,14},{18... | collective-permute-start | bytes 1179656 | tf_op jit(solution)/shard_map/ppermute | solution.py:19
  19.5 16.6 %collective-permute-start.1 = (bf16[2,256,384]{2,1,0:T(8,128)(2,1)}, bf16[2,256,384]{2,1,0:T(8,128)(2,1)}, u32[]{:S(2)}, u32[]{:S(2)}) collective-permute-start(bf16[2,256,384]{2,1,0:T(8,128)(2,1)} %slice.450), channel_id=1, source_target_pairs={{0,112},{2,114},{4,116},{6,118},{8,120},{10,122},{12,124},{14,126}... | collective-permute-start | bytes 1179656 | tf_op jit(solution)/shard_map/ppermute | solution.py:19
  20.7 12.7 %collective-permute-start.2 = (bf16[2,256,256]{2,1,0:T(8,128)(2,1)}, bf16[2,256,256]{2,1,0:T(8,128)(2,1)}, u32[]{:S(2)}, u32[]{:S(2)}) collective-permute-start(bf16[2,256,256]{2,1,0:T(8,128)(2,1)} %slice.451), channel_id=1, source_target_pairs={{0,110},{2,112},{4,114},{6,116},{8,118},{10,120},{12,122},{14,124}... | collective-permute-start | bytes 786440 | tf_op jit(solution)/shard_map/ppermute | solution.py:19
  24.1 44.8 %copy-start.27 = (bf16[256,256]{1,0:T(8,128)(2,1)}, bf16[256,256]{1,0:T(8,128)(2,1)S(1)}, u32[]{:S(2)}) copy-start(bf16[256,256]{1,0:T(8,128)(2,1)S(1)} %multiply_convert_fusion.2) | copy-start | bytes 393220
  73.5 168.7 %all-reduce.9.cloned.1.call-start = ((), (), s32[]{:S(2)}) async-start(), calls=%async_computation.1 | async-start | bytes 1179648 | tf_op jit(solution)/shard_map/psum | solution.py:147
  74.4 32.1 %copy-start.38 = (f32[4]{0:T(128)}, f32[4]{0:T(128)S(1)}, u32[]{:S(2)}) copy-start(f32[4]{0:T(128)S(1)} %compare_convert_fusion) | copy-start | bytes 52
  75.4 41.9 %copy-start.35 = (bf16[256,256]{1,0:T(8,128)(2,1)}, bf16[256,256]{1,0:T(8,128)(2,1)S(1)}, u32[]{:S(2)}) copy-start(bf16[256,256]{1,0:T(8,128)(2,1)S(1)} %get-tuple-element.334) | copy-start | bytes 393220
  75.4 49.0 %copy-start.29 = (bf16[256,256]{1,0:T(8,128)(2,1)}, bf16[256,256]{1,0:T(8,128)(2,1)S(1)}, u32[]{:S(2)}) copy-start(bf16[256,256]{1,0:T(8,128)(2,1)S(1)} %get-tuple-element.335) | copy-start | bytes 393220
  181.3 17.4 %copy-start.3 = (f32[2,640,640]{2,1,0:T(8,128)S(1)}, f32[2,640,640]{2,1,0:T(8,128)}, u32[]{:S(2)}) copy-start(f32[2,640,640]{2,1,0:T(8,128)} %get-tuple-element.232) | copy-start | bytes 9830404
  183.6 15.1 %collective-permute-start.3 = (bf16[2,256,384]{2,1,0:T(8,128)(2,1)S(1)}, bf16[2,256,384]{2,1,0:T(8,128)(2,1)S(1)}, u32[]{:S(2)}, u32[]{:S(2)}) collective-permute-start(bf16[2,256,384]{2,1,0:T(8,128)(2,1)S(1)} %slice.463), channel_id=1, source_target_pairs={{0,16},{2,18},{4,20},{6,22},{8,24},{10,26},{12,28},{14,30},{16,32}... | collective-permute-start | bytes 1179656 | tf_op jit(solution)/shard_map/ppermute | solution.py:19
  186.7 19.6 %collective-permute-start.4 = (bf16[2,256,256]{2,1,0:T(8,128)(2,1)S(1)}, bf16[2,256,256]{2,1,0:T(8,128)(2,1)S(1)}, u32[]{:S(2)}, u32[]{:S(2)}) collective-permute-start(bf16[2,256,256]{2,1,0:T(8,128)(2,1)S(1)} %slice.465), channel_id=1, source_target_pairs={{0,18},{2,20},{4,22},{6,24},{8,26},{10,28},{12,30},{14,32},{16,34}... | collective-permute-start | bytes 786440 | tf_op jit(solution)/shard_map/ppermute | solution.py:19
  206.3 16.1 %copy-start.24 = (f32[2,256,256]{2,1,0:T(8,128)S(1)}, f32[2,256,256]{2,1,0:T(8,128)}, u32[]{:S(2)}) copy-start(f32[2,256,256]{2,1,0:T(8,128)} %get-tuple-element.253) | copy-start | bytes 1572868
  206.4 15.1 %collective-permute-start.5 = (bf16[2,384,256]{2,1,0:T(8,128)(2,1)S(1)}, bf16[2,384,256]{2,1,0:T(8,128)(2,1)S(1)}, u32[]{:S(2)}, u32[]{:S(2)}) collective-permute-start(bf16[2,384,256]{2,1,0:T(8,128)(2,1)S(1)} %slice.531), channel_id=1, source_target_pairs={{0,2},{2,4},{4,6},{6,8},{8,10},{10,12},{12,14},{14,16},{16,18},{18... | collective-permute-start | bytes 1179656 | tf_op jit(solution)/shard_map/ppermute | solution.py:19
  221.6 20.7 %copy-start.4 = (f32[1,2,384,384]{3,2,1,0:T(8,128)S(1)}, f32[1,2,384,384]{3,2,1,0:T(8,128)}, u32[]{:S(2)}) copy-start(f32[1,2,384,384]{3,2,1,0:T(8,128)} %param.23) | copy-start | bytes 3538948
  222.4 160.7 %all-reduce.11.cloned.1.call-start = ((), (), s32[]{:S(2)}) async-start(), calls=%async_computation.2 | async-start | bytes 2097152 | tf_op jit(solution)/shard_map/psum | solution.py:148
  223.5 159.6 %copy-start.7 = (f32[2,2,256,256]{3,2,1,0:T(8,128)S(1)}, f32[2,2,256,256]{3,2,1,0:T(8,128)}, u32[]{:S(2)}) copy-start(f32[2,2,256,256]{3,2,1,0:T(8,128)} %param.24) | copy-start | bytes 3145732
  223.5 240.8 %all-reduce.13.cloned.1.call-start = ((), (), s32[]{:S(2)}) async-start(), calls=%async_computation.3 | async-start | bytes 1048576 | tf_op jit(solution)/shard_map/psum | solution.py:114
  245.1 147.4 %collective-permute-start.6 = (bf16[2,384,256]{2,1,0:T(8,128)(2,1)}, bf16[2,384,256]{2,1,0:T(8,128)(2,1)S(1)}, u32[]{:S(2)}, u32[]{:S(2)}) collective-permute-start(bf16[2,384,256]{2,1,0:T(8,128)(2,1)} %slice.470), channel_id=1, source_target_pairs={{0,126},{2,0},{4,2},{6,4},{8,6},{10,8},{12,10},{14,12},{16,14},{18... | collective-permute-start | bytes 1179656 | tf_op jit(solution)/shard_map/ppermute | solution.py:19
  252.2 141.8 %collective-permute-start.7 = (bf16[2,256,384]{2,1,0:T(8,128)(2,1)}, bf16[2,256,384]{2,1,0:T(8,128)(2,1)}, u32[]{:S(2)}, u32[]{:S(2)}) collective-permute-start(bf16[2,256,384]{2,1,0:T(8,128)(2,1)} %slice.471), channel_id=1, source_target_pairs={{0,112},{2,114},{4,116},{6,118},{8,120},{10,122},{12,124},{14,126}... | collective-permute-start | bytes 1179656 | tf_op jit(solution)/shard_map/ppermute | solution.py:19
  384.6 7.9 %collective-permute-start.8 = (bf16[2,256,256]{2,1,0:T(8,128)(2,1)S(1)}, bf16[2,256,256]{2,1,0:T(8,128)(2,1)S(1)}, u32[]{:S(2)}, u32[]{:S(2)}) collective-permute-start(bf16[2,256,256]{2,1,0:T(8,128)(2,1)S(1)} %slice.472), channel_id=1, source_target_pairs={{0,110},{2,112},{4,114},{6,116},{8,118},{10,120},{12,122},{14,124}... | collective-permute-start | bytes 786440 | tf_op jit(solution)/shard_map/ppermute | solution.py:19
  435.8 28.5 %copy-start.39 = (f32[4]{0:T(128)S(1)}, f32[4]{0:T(128)}, u32[]{:S(2)}) copy-start(f32[4]{0:T(128)} %copy-done.38) | copy-start | bytes 52
  436.9 248.0 %all-reduce.17.cloned.1.call-start = ((), (), s32[]{:S(2)}) async-start(), calls=%async_computation.5 | async-start | bytes 2097152 | tf_op jit(solution)/shard_map/psum | solution.py:148
  541.8 16.2 %copy-start.2 = (f32[2,640,640]{2,1,0:T(8,128)S(1)}, f32[2,640,640]{2,1,0:T(8,128)}, u32[]{:S(2)}) copy-start(f32[2,640,640]{2,1,0:T(8,128)} %get-tuple-element.233) | copy-start | bytes 9830404
  542.6 15.4 %collective-permute-start.9 = (bf16[2,256,384]{2,1,0:T(8,128)(2,1)}, bf16[2,256,384]{2,1,0:T(8,128)(2,1)}, u32[]{:S(2)}, u32[]{:S(2)}) collective-permute-start(bf16[2,256,384]{2,1,0:T(8,128)(2,1)} %slice.484), channel_id=1, source_target_pairs={{0,16},{2,18},{4,20},{6,22},{8,24},{10,26},{12,28},{14,30},{16,32}... | collective-permute-start | bytes 1179656 | tf_op jit(solution)/shard_map/ppermute | solution.py:19
  546.7 165.5 %all-reduce.15.cloned.1.call-start = ((), (), s32[]{:S(2)}) async-start(), calls=%async_computation.4 | async-start | bytes 1179648 | tf_op jit(solution)/shard_map/psum | solution.py:147
  546.8 19.6 %collective-permute-start.10 = (bf16[2,256,256]{2,1,0:T(8,128)(2,1)S(1)}, bf16[2,256,256]{2,1,0:T(8,128)(2,1)S(1)}, u32[]{:S(2)}, u32[]{:S(2)}) collective-permute-start(bf16[2,256,256]{2,1,0:T(8,128)(2,1)S(1)} %slice.486), channel_id=1, source_target_pairs={{0,18},{2,20},{4,22},{6,24},{8,26},{10,28},{12,30},{14,32},{16,34}... | collective-permute-start | bytes 786440 | tf_op jit(solution)/shard_map/ppermute | solution.py:19
  566.5 15.5 %collective-permute-start.11 = (bf16[2,384,256]{2,1,0:T(8,128)(2,1)S(1)}, bf16[2,384,256]{2,1,0:T(8,128)(2,1)S(1)}, u32[]{:S(2)}, u32[]{:S(2)}) collective-permute-start(bf16[2,384,256]{2,1,0:T(8,128)(2,1)S(1)} %slice.530), channel_id=1, source_target_pairs={{0,2},{2,4},{4,6},{6,8},{8,10},{10,12},{12,14},{14,16},{16,18},{18... | collective-permute-start | bytes 1179656 | tf_op jit(solution)/shard_map/ppermute | solution.py:19
  582.9 129.4 %copy-start.5 = (f32[1,2,384,384]{3,2,1,0:T(8,128)S(1)}, f32[1,2,384,384]{3,2,1,0:T(8,128)}, u32[]{:S(2)}) copy-start(f32[1,2,384,384]{3,2,1,0:T(8,128)} %param.23) | copy-start | bytes 3538948
  582.9 129.3 %copy-start.22 = (bf16[2,384,384]{2,1,0:T(8,128)(2,1)S(1)}, bf16[2,384,384]{2,1,0:T(8,128)(2,1)}, u32[]{:S(2)}) copy-start(bf16[2,384,384]{2,1,0:T(8,128)(2,1)} %all-reduce.9.cloned.1.call-done) | copy-start | bytes 1769476
  684.9 29.7 %copy-start.1 = (f32[8,2]{0,1:T(2,128)S(1)}, f32[8,2]{0,1:T(2,128)}, u32[]{:S(2)}) copy-start(f32[8,2]{0,1:T(2,128)} %param.25) | copy-start | bytes 196
  (27 other events, 118.1 us)
Sparse Core Ops, SparseCore 0:
  73.6 30.9 all-reduce.6
  222.5 19.6 all-reduce.8
  247.6 135.4 all-reduce.10
  437.0 27.2 all-reduce.12
  546.8 137.9 all-reduce.16
  687.9 24.2 all-reduce.14
where the time goes:
time: 733 us; the launch traced here: 722 us
  waiting for transfers between devices  407 us (56%)
  local copies, waits for them, and re-layouts  134 us (18%)
  other arithmetic  80.1 us (11%)
  starting transfers between devices  32.2 us (4%)
  loops' own time  30.9 us (4%)
  matrix products  22 us (3%)
  between operations  15.9 us (2%)
    psum x2, waiting for transfers between devices, body(): probe_grad = lax.psum(probe_updates, 'tile')  232 us
    ppermute x12, waiting for transfers between devices, shifted(): lax.ppermute(array, axis, [(i, (i + by) % peers) for i in range(peers)])  74.8 us
    psum x2, waiting for transfers between devices, mode_total(): return lax.psum(part.astype(jnp.bfloat16), 'mode').astype(jnp.float32)  56.3 us
    dynamic_update_slice x8, local copies, waits for them, and re-layouts, place(): return lax.dynamic_update_slice(acc, current + object_terms[slot], where)  51.8 us
    psum x2, waiting for transfers between devices, body(): lax.psum(tile_grad.astype(jnp.bfloat16), 'mode').astype(jnp.float32)  42.9 us
    ppermute x12, starting transfers between devices, shifted(): lax.ppermute(array, axis, [(i, (i + by) % peers) for i in range(peers)])  31.5 us
    another operation x2, loops' own time, body(): gradient = lax.fori_loop(0, object_terms.shape[0], place, gradient)  30.7 us
    another operation x7, other arithmetic  21.3 us
  transfers between devices with their start and end apart: 18, of which 15 were waited for; matrix products, arithmetic and copies ran while one was open for 3% of the time, Pallas kernels for 0%

commit v1 on v0

v1 whole, which is shorter than its diff:
```python
import functools

import jax
import jax.numpy as jnp
import numpy as np
from jax import lax
from jax.experimental import pallas as pl
from jax.experimental.pallas import tpu as pltpu
from jax.sharding import PartitionSpec as P

MESH = pl.DeviceIdType.MESH
BF16 = jnp.bfloat16
F32 = jnp.float32
GC = 8
ITERS = 2
TILES = 64
SLOTS = 4
MODES = 2
N = 256
L = 128
TILE = 384
FRAME = 640
STEP_OBJECT = 0.1
STEP_PROBE = 4.0 / 128.0


def dft_tables(sign):
    index = np.arange(N, dtype=np.int64)
    angle = (index[:, None] * index[None, :] % N).astype(np.float32) * np.float32(2.0 * np.pi / N)
    factor = np.float32(1.0 / 16.0)
    real = np.cos(angle) * factor
    imag = np.float32(sign) * np.sin(angle) * factor
    left = np.block([[real, -imag], [imag, real]])
    right = np.block([[real, imag], [-imag, real]])
    return jnp.asarray(left, BF16), jnp.asarray(right, BF16)


def kernel(
    obj_ref, probe_ref, mw_ref, meas_ref, corner_ref, counts_ref, widx_ref,
    fl_ref, fr_ref, gl_ref, gr_ref,
    objo_ref, probeo_ref,
    frame, ob, h_right, h_below, h_diag,
    patches, psi, inten, ipart_s, ipart_r, terms, pgrad, zall,
    g_send, g_recv, g_own, margin, m_right, m_below, m_diag,
    rs_send, rs_recv, ag_mine, ag_recv,
    s_halo, r_halo, s_fwd, r_fwd, s_int, r_int, s_g, r_g, s_m, r_m,
    s_rs, r_rs, s_ag, r_ag, s_obj, r_obj,
):
    t = lax.axis_index("tile")
    k = lax.axis_index("mode")
    other = 1 - k

    def away(by):
        return lax.rem(t + (TILES + by) % TILES, TILES)

    def remote(src, dst, ssem, rsem, tile, core):
        return pltpu.make_async_remote_copy(
            src_ref=src, dst_ref=dst, send_sem=ssem, recv_sem=rsem,
            device_id=(tile, core), device_id_type=MESH,
        )

    barrier = pltpu.get_barrier_semaphore()

    def greet(p, _):
        pl.semaphore_signal(barrier, inc=1, device_id=(lax.rem(t + p, TILES), k), device_id_type=MESH)
        return 0

    lax.fori_loop(1, TILES, greet, 0)
    pl.semaphore_signal(barrier, inc=1, device_id=(t, other), device_id_type=MESH)

    probeo_ref[...] = probe_ref[...]
    objo_ref[...] = obj_ref[...]
    for c in range(2):
        for j in range(3):
            ob[c, j] = obj_ref[0, c, :, j * L:(j + 1) * L].astype(BF16)
    zall[0] = jnp.zeros((1024, L), F32)

    def clear(i, _):
        zall[i, 0:TILE] = jnp.zeros((TILE, L), F32)
        zall[i, FRAME:1024] = jnp.zeros((1024 - FRAME, L), F32)
        return 0

    lax.fori_loop(1, 25, clear, 0)
    pl.semaphore_wait(barrier, TILES)

    lane = lax.broadcasted_iota(jnp.int32, (N, L), 1)

    def sweep(it, _):
        halos = (
            (ob.at[k, pl.ds(0, 2)], h_right, away(-1)),
            (ob.at[k, :, pl.ds(0, N)], h_below, away(-GC)),
            (ob.at[k, pl.ds(0, 2), pl.ds(0, N)], h_diag, away(-GC - 1)),
        )
        sends = [
            remote(src, dst.at[k], s_halo.at[i], r_halo.at[i], to, k)
            for i, (src, dst, to) in enumerate(halos)
        ]
        for send in sends:
            send.start()
        forwards = []
        for i, (src, dst, to) in enumerate(halos):
            sends[i].wait()
            forward = remote(dst.at[k], dst.at[k], s_fwd.at[i], r_fwd.at[i], t, other)
            forward.start()
            forwards.append(forward)
        for c in range(2):
            for j in range(3):
                frame[c, j, 0:TILE] = ob[c, j].astype(F32)
        for forward in forwards:
            forward.wait()
        for c in range(2):
            for j in range(2):
                frame[c, 3 + j, 0:TILE] = h_right[c, j].astype(F32)
                frame[c, 3 + j, TILE:FRAME] = h_diag[c, j].astype(F32)
            for j in range(3):
                frame[c, j, TILE:FRAME] = h_below[c, j].astype(F32)

        def intensity_copy(s):
            return remote(ipart_s.at[s], ipart_r.at[s], s_int.at[s], r_int.at[s], t, other)

        def forward_slot(s, _):
            row = corner_ref[s, 0]
            col = corner_ref[s, 1]
            q = lax.div(col, L)
            rem = lax.rem(col, L)
            back = lax.rem(L - rem, L)
            for c in range(2):
                rolled = [
                    pltpu.roll(frame[c, q + j, pl.ds(row, N), :], back, 1) for j in range(3)
                ]
                for j in range(2):
                    patches[s, c, :, j * L:(j + 1) * L] = jnp.where(
                        lane < L - rem, rolled[j], rolled[j + 1]
                    )
            o_re = patches[s, 0]
            o_im = patches[s, 1]
            total = None
            for m in range(MODES):
                p_re = probeo_ref[m, 0]
                p_im = probeo_ref[m, 1]
                e_re = (p_re * o_re - p_im * o_im).astype(BF16)
                e_im = (p_re * o_im + p_im * o_re).astype(BF16)
                first = jnp.dot(
                    fl_ref[...], jnp.concatenate([e_re, e_im], 0), preferred_element_type=F32
                ).astype(BF16)
                first = jnp.concatenate([first[:N], first[N:]], 1)
                wave = jnp.dot(first, fr_ref[...], preferred_element_type=F32)
                psi[s, m] = wave
                w = mw_ref[widx_ref[s], m]
                part = w * (wave[:, :N] * wave[:, :N] + wave[:, N:] * wave[:, N:])
                total = part if total is None else total + part
            inten[s] = total
            ipart_s[s] = total.astype(BF16)
            intensity_copy(s).start()
            return 0

        lax.fori_loop(0, SLOTS, forward_slot, 0)

        def scatter_copy(m, p):
            peer = lax.rem(t + p, TILES)
            return remote(
                rs_send.at[m, pl.ds(peer * 16, 16)], rs_recv.at[m, pl.ds(p * 16, 16)],
                s_rs.at[m], r_rs.at[m], peer, k,
            )

        def gather_copy(m, p):
            peer = lax.rem(t + p, TILES)
            return remote(
                ag_mine.at[m], ag_recv.at[m, pl.ds(t * 16, 16)], s_ag.at[m], r_ag.at[m], peer, k
            )

        for m in range(MODES):
            pgrad[...] = jnp.zeros_like(pgrad)

            def backward_slot(s, _):
                w = mw_ref[widx_ref[s], m]
                if m == 0:
                    intensity_copy(s).wait()
                    live = jnp.where(s < counts_ref[0], 1.0, 0.0).astype(F32)
                    inten[s] = (inten[s] + ipart_r[s].astype(F32) - meas_ref[s]) * live
                factor = w * inten[s]
                s_re = (factor * psi[s, m, :, 0:N]).astype(BF16)
                s_im = (factor * psi[s, m, :, N:2 * N]).astype(BF16)
                first = jnp.dot(
                    gl_ref[...], jnp.concatenate([s_re, s_im], 0), preferred_element_type=F32
                ).astype(BF16)
                first = jnp.concatenate([first[:N], first[N:]], 1)
                chi = jnp.dot(first, gr_ref[...], preferred_element_type=F32)
                c_re = chi[:, :N]
                c_im = chi[:, N:]
                p_re = probeo_ref[m, 0]
                p_im = probeo_ref[m, 1]
                o_re = patches[s, 0]
                o_im = patches[s, 1]
                t_re = p_re * c_re + p_im * c_im
                t_im = p_re * c_im - p_im * c_re
                if m == 0:
                    terms[s, 0] = t_re
                    terms[s, 1] = t_im
                else:
                    terms[s, 0] = terms[s, 0] + t_re
                    terms[s, 1] = terms[s, 1] + t_im
                pgrad[0] = pgrad[0] + o_re * c_re + o_im * c_im
                pgrad[1] = pgrad[1] + o_re * c_im - o_im * c_re
                return 0

            lax.fori_loop(0, SLOTS, backward_slot, 0)
            for c in range(2):
                for j in range(2):
                    rs_send[m, (c * 2 + j) * N:(c * 2 + j + 1) * N] = pgrad[
                        c, :, j * L:(j + 1) * L
                    ].astype(BF16)

            def scatter(p, _):
                scatter_copy(m, p).start()
                return 0

            lax.fori_loop(1, TILES, scatter, 0)

        def spread(s, _):
            rem = lax.rem(corner_ref[s, 1], L)
            for c in range(2):
                left = pltpu.roll(terms[s, c, :, 0:L], rem, 1)
                right = pltpu.roll(terms[s, c, :, L:2 * L], rem, 1)
                base = 1 + (s * 2 + c) * 3
                zall[base, TILE:FRAME] = jnp.where(lane >= rem, left, 0.0)
                zall[base + 1, TILE:FRAME] = jnp.where(lane >= rem, right, left)
                zall[base + 2, TILE:FRAME] = jnp.where(lane >= rem, 0.0, right)
            return 0

        lax.fori_loop(0, SLOTS, spread, 0)

        rows_block = 128

        def place(c, j, b):
            total = None
            for s in range(SLOTS):
                d = j - lax.div(corner_ref[s, 1], L)
                inside = jnp.logical_and(d >= 0, d <= 2)
                index = jnp.where(inside, 1 + (s * 2 + c) * 3 + d, 0)
                start = TILE - corner_ref[s, 0] + b * rows_block
                part = zall[index, pl.ds(start, rows_block), :]
                total = part if total is None else total + part
            return total

        def place_send(i, _):
            j = lax.div(i, 5)
            b = lax.rem(i, 5)
            rows = pl.ds(pl.multiple_of(b * rows_block, rows_block), rows_block)
            g_send[j, rows, :] = place(other, j, b).astype(BF16)
            return 0

        lax.fori_loop(0, 25, place_send, 0)
        pair = remote(g_send, g_recv, s_g, r_g, t, other)
        pair.start()

        def place_own(i, _):
            j = lax.div(i, 5)
            b = lax.rem(i, 5)
            rows = pl.ds(pl.multiple_of(b * rows_block, rows_block), rows_block)
            g_own[j, rows, :] = place(k, j, b)
            return 0

        lax.fori_loop(0, 25, place_own, 0)
        pair.wait()
        for j in range(5):
            total = g_own[j] + g_recv[j].astype(F32)
            g_own[j] = total
            margin[j] = total.astype(BF16)
        margins = (
            (margin.at[pl.ds(3, 2), pl.ds(0, TILE)], m_right, away(1)),
            (margin.at[pl.ds(0, 3), pl.ds(TILE, N)], m_below, away(GC)),
            (margin.at[pl.ds(3, 2), pl.ds(TILE, N)], m_diag, away(GC + 1)),
        )
        sends = [
            remote(src, dst, s_m.at[i], r_m.at[i], to, k)
            for i, (src, dst, to) in enumerate(margins)
        ]
        for send in sends:
            send.start()

        def gather(m):
            whole = remote(
                rs_send.at[m, pl.ds(16, 63 * 16)], rs_recv.at[m, pl.ds(16, 63 * 16)],
                s_rs.at[m], r_rs.at[m], away(1), k,
            )
            whole.wait()
            total = rs_send[m, pl.ds(pl.multiple_of(t * 16, 16), 16), :].astype(F32)
            rest = rs_recv[m, 16:64 * 16].astype(F32).reshape(63, 16, L)
            total = (total + jnp.sum(rest, 0)).astype(BF16)
            ag_mine[m] = total
            ag_recv[m, pl.ds(pl.multiple_of(t * 16, 16), 16), :] = total

            def one(p, _):
                gather_copy(m, p).start()
                return 0

            lax.fori_loop(1, TILES, one, 0)

        for m in range(MODES):
            gather(m)

        for send in sends:
            send.wait()
        for j in range(3):
            total = g_own[j, 0:TILE]
            below = m_below[j].astype(F32)
            if j < 2:
                below = below + m_diag[j].astype(F32)
            total = total + jnp.concatenate([below, jnp.zeros((TILE - N, L), F32)], 0)
            if j < 2:
                total = total + m_right[j].astype(F32)
            now = objo_ref[0, k, :, j * L:(j + 1) * L] - STEP_OBJECT * total
            objo_ref[0, k, :, j * L:(j + 1) * L] = now
            ob[k, j] = now.astype(BF16)
        share = remote(ob.at[k], ob.at[k], s_fwd.at[3], r_fwd.at[3], t, other)
        share.start()

        for m in range(MODES):
            remote(
                rs_send.at[m, pl.ds(16, 63 * 16)], ag_recv.at[m, pl.ds(16, 63 * 16)],
                s_ag.at[m], r_ag.at[m], away(1), k,
            ).wait()
            for c in range(2):
                for j in range(2):
                    grad = ag_recv[m, (c * 2 + j) * N:(c * 2 + j + 1) * N].astype(F32)
                    cols = slice(j * L, (j + 1) * L)
                    probeo_ref[m, c, :, cols] = probeo_ref[m, c, :, cols] - STEP_PROBE * grad
        share.wait()
        return 0

    lax.fori_loop(0, ITERS, sweep, 0)
    last = remote(objo_ref.at[0, k], objo_ref.at[0, k], s_obj, r_obj, t, other)
    last.start()
    last.wait()


def body(obj, probe, mode_weights, measured, corner, counts, weight_index):
    vmem = pl.BlockSpec(memory_space=pltpu.VMEM)
    smem = pl.BlockSpec(memory_space=pltpu.SMEM)
    dma = pltpu.SemaphoreType.DMA
    return pl.pallas_call(
        kernel,
        name="ptycho",
        out_shape=(
            jax.ShapeDtypeStruct(obj.shape, F32),
            jax.ShapeDtypeStruct(probe.shape, F32),
        ),
        in_specs=[vmem, vmem, smem, vmem, smem, smem, smem, vmem, vmem, vmem, vmem],
        out_specs=(vmem, vmem),
        scratch_shapes=[
            pltpu.VMEM((2, 5, FRAME, L), F32),
            pltpu.VMEM((2, 3, TILE, L), BF16),
            pltpu.VMEM((2, 2, TILE, L), BF16),
            pltpu.VMEM((2, 3, N, L), BF16),
            pltpu.VMEM((2, 2, N, L), BF16),
            pltpu.VMEM((SLOTS, 2, N, N), F32),
            pltpu.VMEM((SLOTS, MODES, N, 2 * N), F32),
            pltpu.VMEM((SLOTS, N, N), F32),
            pltpu.VMEM((SLOTS, N, N), BF16),
            pltpu.VMEM((SLOTS, N, N), BF16),
            pltpu.VMEM((SLOTS, 2, N, N), F32),
            pltpu.VMEM((2, N, N), F32),
            pltpu.VMEM((25, 1024, L), F32),
            pltpu.VMEM((5, FRAME, L), BF16),
            pltpu.VMEM((5, FRAME, L), BF16),
            pltpu.VMEM((5, FRAME, L), F32),
            pltpu.VMEM((5, FRAME, L), BF16),
            pltpu.VMEM((2, TILE, L), BF16),
            pltpu.VMEM((3, N, L), BF16),
            pltpu.VMEM((2, N, L), BF16),
            pltpu.VMEM((MODES, 1024, L), BF16),
            pltpu.VMEM((MODES, 1024, L), BF16),
            pltpu.VMEM((MODES, 16, L), BF16),
            pltpu.VMEM((MODES, 1024, L), BF16),
            dma((3,)), dma((3,)), dma((4,)), dma((4,)), dma((4,)), dma((4,)),
            dma, dma, dma((3,)), dma((3,)),
            dma((2,)), dma((2,)), dma((2,)), dma((2,)), dma, dma,
        ],
        compiler_params=pltpu.CompilerParams(
            collective_id=0, has_side_effects=True, vmem_limit_bytes=60 << 20
        ),
    )(obj, probe, mode_weights, measured, corner, counts, weight_index,
      *dft_tables(-1.0), *dft_tables(1.0))


def solution(mesh):
    placed = (
        P("tile", None, None, None),
        P("mode", None, None, None),
        P(None, "mode"),
        P("tile", None, None),
        P("tile", None),
        P("tile"),
        P("tile"),
    )
    return jax.shard_map(
        body,
        mesh=mesh,
        in_specs=placed,
        out_specs=(P("tile", None, None, None), P("mode", None, None, None)),
        check_vma=False,
    )
```

time: 733 us -> 125 us (0.17); the launches traced: 722 us -> 125 us
  waiting for transfers between devices: 407 us -> 0 us
  local copies, waits for them, and re-layouts: 134 us -> 6.1 us
  Pallas kernels: 0 us -> 118 us
  other arithmetic: 80.1 us -> 0 us
  starting transfers between devices: 32.2 us -> 0 us
  loops' own time: 30.9 us -> 0 us
  matrix products: 22 us -> 0 us
  between operations: 15.9 us -> 1.29 us
    psum x6 -> x0, waiting for transfers between devices: 332 us -> none  [the longest x2 232 us: body(): probe_grad = lax.psum(probe_updates, 'tile')]
    pallas_call x0 -> x1, Pallas kernels: none -> 118 us  [body(): pl.pallas_call(kernel, name='ptycho', out_shape=(jax.ShapeDtypeStruct(obj...]
    ppermute x12 -> x0, waiting for transfers between devices: 74.8 us -> none  [shifted(): lax.ppermute(array, axis, [(i, (i + by) % peers) for i in range(peers)])]
    dynamic_update_slice x8 -> x0, local copies, waits for them, and re-layouts: 51.8 us -> none  [place(): return lax.dynamic_update_slice(acc, current + object_terms[slot], where)]
    another operation x13 -> x0, other arithmetic: 33.3 us -> none
    ppermute x12 -> x0, starting transfers between devices: 31.5 us -> none  [shifted(): lax.ppermute(array, axis, [(i, (i + by) % peers) for i in range(peers)])]
    another operation x4 -> x0, loops' own time: 30.9 us -> none  [the longest x2 30.7 us: body(): gradient = lax.fori_loop(0, object_terms.shape[0], place, gradient)]
    dot_general x9 -> x0, matrix products: 22 us -> none  [the longest x4 16.8 us: transform(): jnp.einsum('ij,bjk->bik', left, field.reshape(count, 2 * length, length),...]
  transfers between devices with their start and end apart: 18 -> 0, of which waited for: 15 -> 0; matrix products, arithmetic and copies ran while one was open for 3% -> 0% of each run, Pallas kernels for 0% -> 0%
where the time goes in v1:
time: 125 us
  Pallas kernels  118 us (94%)
  local copies, waits for them, and re-layouts  6.1 us (5%)
  between operations  1.29 us (1%)
    pallas_call x1, Pallas kernels, body(): pl.pallas_call(kernel, name='ptycho', out_shape=(jax.ShapeDtypeStruct(obj...  118 us
    unnamed x6, local copies, waits for them, and re-layouts  6.1 us

profile of v1, /device:TPU:1, one launch (start us, length us, event | category | flops | bytes accessed | tf_op | source)
XLA Modules:
  0.0 125.2 jit_solution(6001992444650152517)
XLA Ops:
  1.3 1.3 %copy.14.corner_ref = s32[4,2]{1,0:T(4,128)} copy(s32[4,2]{0,1:T(2,128)} %param.15) | data formatting | bytes 64 | tf_op args[4]
  2.6 1.3 %copy.13.mw_ref = f32[8,2]{1,0:T(8,128)} copy(f32[8,2]{0,1:T(2,128)} %param.13) | data formatting | bytes 128 | tf_op args[2]
  4.0 117.8 %ptycho.1 = (f32[1,2,384,384]{3,2,1,0:T(8,128)}, f32[2,2,256,256]{3,2,1,0:T(8,128)}) custom-call(f32[1,2,384,384]{3,2,1,0:T(8,128)} %obj_ref.1, f32[2,2,256,256]{3,2,1,0:T(8,128)} %probe_ref.1, f32[8,2]{1,0:T(8,128)} %copy.13.mw_ref, f32[4,256,256]{2,1,0:T(8,128)} %meas_ref.1, s32[4,2]{1,0:T(4,128)} %copy.14.corner_ref, s32[1]{0:T(128)S(6)} %copy.17.counts_ref, ...), custom_call_target="tpu_custom_call" | custom-call | tf_op jit(solution)/shard_map/ptycho/pallas_call | solution.py:342
  121.8 0.0 copy-start
  121.8 2.4 %copy.18 = f32[1,2,384,384]{3,2,1,0:T(8,128)} copy(f32[1,2,384,384]{3,2,1,0:T(8,128)} %get-tuple-element.4) | data formatting | bytes 2359296
  124.2 0.0 copy-done
  124.2 1.0 copy.19
Async XLA Ops:
  121.8 2.5 %copy-start = (f32[2,2,256,256]{3,2,1,0:T(8,128)S(1)}, f32[2,2,256,256]{3,2,1,0:T(8,128)}, u32[]{:S(2)}) copy-start(f32[2,2,256,256]{3,2,1,0:T(8,128)} %get-tuple-element.5) | copy-start | bytes 3145732

commit v2 on v1

v2 whole, which is shorter than its diff:
```python
import functools

import jax
import jax.numpy as jnp
import numpy as np
from jax import lax
from jax.experimental import pallas as pl
from jax.experimental.pallas import tpu as pltpu
from jax.sharding import PartitionSpec as P

MESH = pl.DeviceIdType.MESH
BF16 = jnp.bfloat16
F32 = jnp.float32
GC = 8
ITERS = 2
TILES = 64
SLOTS = 4
MODES = 2
N = 256
L = 128
TILE = 384
FRAME = 640
STEP_OBJECT = 0.1
STEP_PROBE = 4.0 / 128.0


def dft_tables():
    index = np.arange(N, dtype=np.int64)
    angle = (index[:, None] * index[None, :] % N).astype(np.float32) * np.float32(2.0 * np.pi / N)
    factor = np.float32(1.0 / 16.0)
    real = np.cos(angle) * factor
    imag = -np.sin(angle) * factor
    one = np.block([[real, -imag], [imag, real]])
    two = np.block([[real, imag], [-imag, real]])
    return jnp.asarray(one, BF16), jnp.asarray(two, BF16)


def kernel(
    obj_hbm, probe_hbm, mw_ref, meas_hbm, corner_ref, counts_ref, widx_ref, one_hbm, two_hbm,
    obj_out, gobj, probe_out, gprobe,
    objs, probes, meas, one, two,
    frame, ob, h_right, h_below, h_diag,
    patches, psi, inten, ipart_s, ipart_r, terms, pgrad, zall,
    g_send, g_recv, g_own, margin, m_right, m_below, m_diag,
    rs_send, rs_recv, ag_mine,
    s_in, s_out, s_halo, r_halo, s_fwd, r_fwd, s_int, r_int, s_g, r_g, s_m, r_m,
    s_rs, r_rs, s_ag, r_ag, s_share, r_share, stage_y, stage_z,
):
    t = lax.axis_index("tile")
    k = lax.axis_index("mode")
    other = 1 - k

    def away(by):
        return lax.rem(t + (TILES + by) % TILES, TILES)

    def along(axis, by):
        size = 4 ** axis
        digit = lax.rem(lax.div(t, size), 4)
        return t + (lax.rem(digit + by, 4) - digit) * size

    def remote(src, dst, ssem, rsem, tile, core):
        return pltpu.make_async_remote_copy(
            src_ref=src, dst_ref=dst, send_sem=ssem, recv_sem=rsem,
            device_id=(tile, core), device_id_type=MESH,
        )

    def signal(sem, tile, core):
        pl.semaphore_signal(sem, inc=1, device_id=(tile, core), device_id_type=MESH)

    loads = [
        pltpu.make_async_copy(src, dst, s_in.at[i])
        for i, (src, dst) in enumerate(
            ((obj_hbm.at[0], objs), (probe_hbm, probes), (one_hbm, one), (two_hbm, two), (meas_hbm, meas))
        )
    ]
    loads[0].start()

    barrier = pltpu.get_barrier_semaphore()
    signal(barrier, t, other)
    for by in (1, GC, GC + 1):
        signal(barrier, away(by), k)
        signal(barrier, away(-by), k)
    for axis in range(3):
        for by in (1, 2, 3):
            signal(barrier, along(axis, by), k)
    for load in loads[1:]:
        load.start()

    loads[0].wait()
    for j in range(3):
        ob[j] = objs[k, :, j * L:(j + 1) * L].astype(BF16)
    pl.semaphore_wait(barrier, 16)

    lane = lax.broadcasted_iota(jnp.int32, (N, L), 1)

    def halo_chunks():
        for j in range(2):
            yield ob.at[j], h_right.at[k, j], away(-1)
        for j in range(3):
            yield ob.at[j, pl.ds(0, N)], h_below.at[k, j], away(-GC)
        for j in range(2):
            yield ob.at[j, pl.ds(0, N)], h_diag.at[k, j], away(-GC - 1)

    halo_sends = [
        remote(src, dst, s_halo.at[i], r_halo.at[i], to, k)
        for i, (src, dst, to) in enumerate(halo_chunks())
    ]
    halo_forwards = [
        remote(dst, dst, s_fwd.at[i], r_fwd.at[i], t, other)
        for i, (src, dst, to) in enumerate(halo_chunks())
    ]
    halo_order = (0, 2, 1, 3, 4, 5, 6)

    def margin_chunks():
        for j in range(2):
            yield margin.at[3 + j, pl.ds(0, TILE)], m_right.at[j], away(1)
        for j in range(3):
            yield margin.at[j, pl.ds(TILE, N)], m_below.at[j], away(GC)
        for j in range(2):
            yield margin.at[3 + j, pl.ds(TILE, N)], m_diag.at[j], away(GC + 1)

    margin_sends = [
        remote(src, dst, s_m.at[i], r_m.at[i], to, k)
        for i, (src, dst, to) in enumerate(margin_chunks())
    ]

    for i in halo_order:
        halo_sends[i].start()

    for by in (1, 2, 3):
        signal(stage_y, along(0, by), k)
    zall[0] = jnp.zeros((1024, L), F32)

    def clear(i, _):
        zall[i, 0:TILE] = jnp.zeros((TILE, L), F32)
        zall[i, FRAME:1024] = jnp.zeros((1024 - FRAME, L), F32)
        return 0

    lax.fori_loop(1, 13, clear, 0)
    pl.semaphore_wait(stage_y, 3)
    for by in (1, 2, 3):
        signal(stage_z, along(2, by), k)
    lax.fori_loop(13, 25, clear, 0)
    pl.semaphore_wait(stage_z, 3)
    for load in loads[1:]:
        load.wait()

    def shard(ref, m, tile):
        return ref.at[
            m, lax.div(tile, 32),
            pl.ds(pl.multiple_of(lax.rem(tile, 16) * 16, 16), 16),
            pl.ds(pl.multiple_of(lax.rem(lax.div(tile, 16), 2) * L, L), L),
        ]

    def sweep(it, _):
        for c in range(2):
            for j in range(3):
                frame[c, j, 0:TILE] = objs[c, :, j * L:(j + 1) * L].astype(BF16).astype(F32)
        for i in halo_order:
            halo_sends[i].wait_recv()
            halo_forwards[i].start()

        def settle(c):
            for j in range(2):
                frame[c, 3 + j, 0:TILE] = h_right[c, j].astype(F32)
            for j in range(3):
                frame[c, j, TILE:FRAME] = h_below[c, j].astype(F32)
            for j in range(2):
                frame[c, 3 + j, TILE:FRAME] = h_diag[c, j].astype(F32)

        settle(k)
        for i in halo_order:
            halo_forwards[i].wait()
        settle(other)
        for send in halo_sends:
            send.wait_send()

        def intensity_copy(s):
            return remote(ipart_s.at[s], ipart_r.at[s], s_int.at[s], r_int.at[s], t, other)

        def forward_slot(s, _):
            row = corner_ref[0, s]
            col = corner_ref[1, s]
            q = lax.div(col, L)
            rem = lax.rem(col, L)
            back = lax.rem(L - rem, L)
            for c in range(2):
                rolled = [
                    pltpu.roll(frame[c, q + j, pl.ds(row, N), :], back, 1) for j in range(3)
                ]
                for j in range(2):
                    patches[s, c, :, j * L:(j + 1) * L] = jnp.where(
                        lane < L - rem, rolled[j], rolled[j + 1]
                    )
            o_re = patches[s, 0]
            o_im = patches[s, 1]
            total = None
            for m in range(MODES):
                p_re = probes[m, 0]
                p_im = probes[m, 1]
                e_re = (p_re * o_re - p_im * o_im).astype(BF16)
                e_im = (p_re * o_im + p_im * o_re).astype(BF16)
                first = jnp.dot(
                    one[...], jnp.concatenate([e_re, e_im], 0), preferred_element_type=F32
                ).astype(BF16)
                first = jnp.concatenate([first[:N], first[N:]], 1)
                wave = jnp.dot(first, two[...], preferred_element_type=F32)
                psi[s, m] = wave
                w = mw_ref[m, widx_ref[s]]
                part = w * (wave[:, :N] * wave[:, :N] + wave[:, N:] * wave[:, N:])
                total = part if total is None else total + part
            inten[s] = total
            ipart_s[s] = total.astype(BF16)
            intensity_copy(s).start()
            return 0

        lax.fori_loop(0, SLOTS, forward_slot, 0)

        def scatter_copy(m, p):
            peer = lax.rem(t + p, TILES)
            return remote(
                shard(rs_send, m, peer), rs_recv.at[m, pl.ds(p * 16, 16)],
                s_rs.at[m], r_rs.at[m], peer, k,
            )

        def gather_copy(m, p):
            peer = lax.rem(t + p, TILES)
            return remote(
                ag_mine.at[m], shard(gprobe, m, t), s_ag.at[m], r_ag.at[m], peer, k
            )

        for m in range(MODES):
            pgrad[...] = jnp.zeros_like(pgrad)

            def backward_slot(s, _):
                w = mw_ref[m, widx_ref[s]]
                if m == 0:
                    intensity_copy(s).wait()
                    live = jnp.where(s < counts_ref[0], 1.0, 0.0).astype(F32)
                    inten[s] = (inten[s] + ipart_r[s].astype(F32) - meas[s]) * live
                factor = w * inten[s]
                s_re = (factor * psi[s, m, :, 0:N]).astype(BF16)
                s_im = (factor * psi[s, m, :, N:2 * N]).astype(BF16)
                first = jnp.dot(
                    two[...], jnp.concatenate([s_re, s_im], 0), preferred_element_type=F32
                ).astype(BF16)
                first = jnp.concatenate([first[:N], first[N:]], 1)
                chi = jnp.dot(first, one[...], preferred_element_type=F32)
                c_re = chi[:, :N]
                c_im = chi[:, N:]
                p_re = probes[m, 0]
                p_im = probes[m, 1]
                o_re = patches[s, 0]
                o_im = patches[s, 1]
                t_re = p_re * c_re + p_im * c_im
                t_im = p_re * c_im - p_im * c_re
                if m == 0:
                    terms[s, 0] = t_re
                    terms[s, 1] = t_im
                else:
                    terms[s, 0] = terms[s, 0] + t_re
                    terms[s, 1] = terms[s, 1] + t_im
                pgrad[0] = pgrad[0] + o_re * c_re + o_im * c_im
                pgrad[1] = pgrad[1] + o_re * c_im - o_im * c_re
                return 0

            lax.fori_loop(0, SLOTS, backward_slot, 0)
            rs_send[m] = pgrad[...].astype(BF16)

            def scatter(p, _):
                scatter_copy(m, p).start()
                return 0

            lax.fori_loop(1, TILES, scatter, 0)

        def spread(s, _):
            rem = lax.rem(corner_ref[1, s], L)
            for c in range(2):
                left = pltpu.roll(terms[s, c, :, 0:L], rem, 1)
                right = pltpu.roll(terms[s, c, :, L:2 * L], rem, 1)
                base = 1 + (s * 2 + c) * 3
                zall[base, TILE:FRAME] = jnp.where(lane >= rem, left, 0.0)
                zall[base + 1, TILE:FRAME] = jnp.where(lane >= rem, right, left)
                zall[base + 2, TILE:FRAME] = jnp.where(lane >= rem, 0.0, right)
            return 0

        lax.fori_loop(0, SLOTS, spread, 0)

        rows_block = 128

        def place(c, j, b):
            total = None
            for s in range(SLOTS):
                d = j - lax.div(corner_ref[1, s], L)
                inside = jnp.logical_and(d >= 0, d <= 2)
                index = jnp.where(inside, 1 + (s * 2 + c) * 3 + d, 0)
                start = TILE - corner_ref[0, s] + b * rows_block
                part = zall[index, pl.ds(start, rows_block), :]
                total = part if total is None else total + part
            return total

        def block(b):
            return pl.ds(pl.multiple_of(b * rows_block, rows_block), rows_block)

        def place_send(i, _):
            j = lax.div(i, 5)
            b = lax.rem(i, 5)
            g_send[j, block(b), :] = place(other, j, b).astype(BF16)
            return 0

        pairs = [
            remote(g_send.at[js], g_recv.at[js], s_g.at[i], r_g.at[i], t, other)
            for i, js in enumerate((pl.ds(3, 2), pl.ds(0, 3)))
        ]
        lax.fori_loop(15, 25, place_send, 0)
        pairs[0].start()
        lax.fori_loop(0, 15, place_send, 0)
        pairs[1].start()

        def place_margin(j, b):
            margin[j, block(b), :] = (
                place(k, j, b) + g_recv[j, block(b), :].astype(F32)
            ).astype(BF16)

        def place_right(i, _):
            place_margin(3 + lax.div(i, 5), lax.rem(i, 5))
            return 0

        def place_below(i, _):
            place_margin(lax.div(i, 2), 3 + lax.rem(i, 2))
            return 0

        def place_tile(i, _):
            j = lax.div(i, 3)
            b = lax.rem(i, 3)
            g_own[j, block(b), :] = place(k, j, b) + g_recv[j, block(b), :].astype(F32)
            return 0

        pairs[0].wait()
        lax.fori_loop(0, 10, place_right, 0)
        for i in (5, 6, 0, 1):
            margin_sends[i].start()
        pairs[1].wait()
        lax.fori_loop(0, 6, place_below, 0)
        for i in (2, 3, 4):
            margin_sends[i].start()
        lax.fori_loop(0, 9, place_tile, 0)

        def gather(m):
            whole = rs_recv.at[m, pl.ds(16, 63 * 16)]
            remote(whole, whole, s_rs.at[m], r_rs.at[m], away(1), k).wait()
            own = shard(rs_send, m, t)[...].astype(F32)
            rest = rs_recv[m, 16:64 * 16].astype(F32).reshape(63, 16, L)
            total = (own + jnp.sum(rest, 0)).astype(BF16)
            ag_mine[m] = total
            shard(gprobe, m, t)[...] = total

            def one_copy(p, _):
                gather_copy(m, p).start()
                return 0

            lax.fori_loop(1, TILES, one_copy, 0)

        for m in range(MODES):
            gather(m)

        for send in margin_sends:
            send.wait()
        more = it < ITERS - 1
        for j in range(3):
            cols = slice(j * L, (j + 1) * L)
            upper = g_own[j, 0:N] + m_below[j].astype(F32)
            lower = g_own[j, N:TILE]
            if j < 2:
                upper = upper + m_diag[j].astype(F32) + m_right[j, 0:N].astype(F32)
                lower = lower + m_right[j, N:TILE].astype(F32)
            gobj[0, k, 0:N, cols] = upper.astype(BF16)
            gobj[0, k, N:TILE, cols] = lower.astype(BF16)
        share = remote(gobj.at[0, k], gobj.at[0, k], s_share, r_share, t, other)
        share.start()

        @pl.when(more)
        def _():
            for j in range(3):
                cols = slice(j * L, (j + 1) * L)
                now = objs[k, :, cols] - STEP_OBJECT * gobj[0, k, :, cols].astype(F32)
                objs[k, :, cols] = now
                ob[j] = now.astype(BF16)
            for i in halo_order:
                halo_sends[i].start()

        for m in range(MODES):
            whole = rs_recv.at[m, pl.ds(16, 63 * 16)]
            remote(whole, whole, s_ag.at[m], r_ag.at[m], away(1), k).wait()
        share.wait()

        @pl.when(more)
        def _():
            probes[...] = probes[...] - STEP_PROBE * gprobe[...].astype(F32)
            objs[other] = objs[other] - STEP_OBJECT * gobj[0, other].astype(F32)
            pltpu.make_async_copy(objs, obj_out.at[0], s_out.at[0]).start()
            pltpu.make_async_copy(probes, probe_out, s_out.at[1]).start()

        return 0

    lax.fori_loop(0, ITERS, sweep, 0)
    pltpu.make_async_copy(objs, obj_out.at[0], s_out.at[0]).wait()
    pltpu.make_async_copy(probes, probe_out, s_out.at[1]).wait()


def body(obj, probe, mode_weights, measured, corner, counts, weight_index):
    vmem = pl.BlockSpec(memory_space=pltpu.VMEM)
    smem = pl.BlockSpec(memory_space=pltpu.SMEM)
    hbm = pl.BlockSpec(memory_space=pl.ANY)
    dma = pltpu.SemaphoreType.DMA
    regular = pltpu.SemaphoreType.REGULAR
    obj_1, grad_obj, probe_1, grad_probe = pl.pallas_call(
        kernel,
        name="ptycho",
        out_shape=(
            jax.ShapeDtypeStruct(obj.shape, F32),
            jax.ShapeDtypeStruct(obj.shape, BF16),
            jax.ShapeDtypeStruct(probe.shape, F32),
            jax.ShapeDtypeStruct(probe.shape, BF16),
        ),
        in_specs=[hbm, hbm, smem, hbm, smem, smem, smem, hbm, hbm],
        out_specs=(hbm, vmem, hbm, vmem),
        scratch_shapes=[
            pltpu.VMEM((2, TILE, TILE), F32),
            pltpu.VMEM((MODES, 2, N, N), F32),
            pltpu.VMEM((SLOTS, N, N), F32),
            pltpu.VMEM((2 * N, 2 * N), BF16),
            pltpu.VMEM((2 * N, 2 * N), BF16),
            pltpu.VMEM((2, 5, FRAME, L), F32),
            pltpu.VMEM((3, TILE, L), BF16),
            pltpu.VMEM((2, 2, TILE, L), BF16),
            pltpu.VMEM((2, 3, N, L), BF16),
            pltpu.VMEM((2, 2, N, L), BF16),
            pltpu.VMEM((SLOTS, 2, N, N), F32),
            pltpu.VMEM((SLOTS, MODES, N, 2 * N), F32),
            pltpu.VMEM((SLOTS, N, N), F32),
            pltpu.VMEM((SLOTS, N, N), BF16),
            pltpu.VMEM((SLOTS, N, N), BF16),
            pltpu.VMEM((SLOTS, 2, N, N), F32),
            pltpu.VMEM((2, N, N), F32),
            pltpu.VMEM((25, 1024, L), F32),
            pltpu.VMEM((5, FRAME, L), BF16),
            pltpu.VMEM((5, FRAME, L), BF16),
            pltpu.VMEM((3, TILE, L), F32),
            pltpu.VMEM((5, FRAME, L), BF16),
            pltpu.VMEM((2, TILE, L), BF16),
            pltpu.VMEM((3, N, L), BF16),
            pltpu.VMEM((2, N, L), BF16),
            pltpu.VMEM((MODES, 2, N, N), BF16),
            pltpu.VMEM((MODES, 1024, L), BF16),
            pltpu.VMEM((MODES, 16, L), BF16),
            dma((5,)), dma((2,)), dma((7,)), dma((7,)), dma((7,)), dma((7,)), dma((4,)), dma((4,)),
            dma((2,)), dma((2,)), dma((7,)), dma((7,)),
            dma((2,)), dma((2,)), dma((2,)), dma((2,)), dma, dma, regular, regular,
        ],
        compiler_params=pltpu.CompilerParams(
            collective_id=0, has_side_effects=True, vmem_limit_bytes=60 << 20
        ),
    )(obj, probe, mode_weights.T, measured, corner.T, counts, weight_index, *dft_tables())
    return (
        obj_1 - STEP_OBJECT * grad_obj.astype(F32),
        probe_1 - STEP_PROBE * grad_probe.astype(F32),
    )


def solution(mesh):
    placed = (
        P("tile", None, None, None),
        P("mode", None, None, None),
        P(None, "mode"),
        P("tile", None, None),
        P("tile", None),
        P("tile"),
        P("tile"),
    )
    return jax.shard_map(
        body,
        mesh=mesh,
        in_specs=placed,
        out_specs=(P("tile", None, None, None), P("mode", None, None, None)),
        check_vma=False,
    )
```

time: 125 us -> 118 us (0.944)
  local copies, waits for them, and re-layouts: 6.1 us -> 0.01 us
  Pallas kernels: 118 us -> 113 us
  other arithmetic: 0 us -> 3.74 us
    unnamed x6 -> x4, local copies, waits for them, and re-layouts: 6.1 us -> 0.01 us
    pallas_call x1, Pallas kernels: 118 us -> 113 us  [body(): pl.pallas_call(kernel, name='ptycho', out_shape=(jax.ShapeDtypeStruct(obj...]
    sub x0 -> x2, other arithmetic: none -> 3.74 us  [the longest x1 2.59 us: body(): probe_1 - STEP_PROBE * grad_probe.astype(F32)]
where the time goes in v2:
time: 118 us
  Pallas kernels  113 us (96%)
  other arithmetic  3.74 us (3%)
  between operations  1.3 us (1%)
    pallas_call x1, Pallas kernels, body(): pl.pallas_call(kernel, name='ptycho', out_shape=(jax.ShapeDtypeStruct(obj...  113 us
    sub x1, other arithmetic, body(): probe_1 - STEP_PROBE * grad_probe.astype(F32)  2.59 us

profile of v2, /device:TPU:1, one launch (start us, length us, event | category | flops | bytes accessed | tf_op | source)
XLA Modules:
  0.0 117.6 jit_solution(13110925657742305898)
XLA Ops:
  1.3 112.6 %ptycho.1 = (f32[1,2,384,384]{3,2,1,0:T(8,128)}, bf16[1,2,384,384]{3,2,1,0:T(8,128)(2,1)}, f32[2,2,256,256]{3,2,1,0:T(8,128)}, bf16[2,2,256,256]{3,2,1,0:T(8,128)(2,1)}) custom-call(f32[1,2,384,384]{3,2,1,0:T(8,128)} %obj_hbm.1, f32[2,2,256,256]{3,2,1,0:T(8,128)} %probe_hbm.1, f32[2,8]{1,0:T(2,128)} %bitcast.2, f32[4,256,256]{2,1,0:T(8,128)} %meas_hbm.1, ...), custom_call_target="tpu_custom_call" | custom-call | tf_op jit(solution)/shard_map/ptycho/pallas_call | solution.py:417
  113.9 0.0 copy-start
  113.9 0.0 copy-start.1
  113.9 2.6 %multiply_subtract_fusion.1 = f32[2,2,256,256]{3,2,1,0:T(8,128)} fusion(f32[2,2,256,256]{3,2,1,0:T(8,128)} %get-tuple-element.8, bf16[2,2,256,256]{3,2,1,0:T(8,128)(2,1)} %get-tuple-element.9), kind=kLoop, calls=%fused_computation.1 | loop fusion | flops 786432 | bytes 2621440 | tf_op jit(solution)/shard_map/sub | solution.py:467
  116.5 0.0 copy-done
  116.5 0.0 copy-done.1
  116.5 1.1 multiply_subtract_fusion
Async XLA Ops:
  113.9 2.6 %copy-start = (f32[1,2,384,384]{3,2,1,0:T(8,128)S(1)}, f32[1,2,384,384]{3,2,1,0:T(8,128)}, u32[]{:S(2)}) copy-start(f32[1,2,384,384]{3,2,1,0:T(8,128)} %get-tuple-element.6) | copy-start | bytes 3538948
  113.9 2.6 %copy-start.1 = (bf16[1,2,384,384]{3,2,1,0:T(8,128)(2,1)S(1)}, bf16[1,2,384,384]{3,2,1,0:T(8,128)(2,1)}, u32[]{:S(2)}) copy-start(bf16[1,2,384,384]{3,2,1,0:T(8,128)(2,1)} %get-tuple-element.7) | copy-start | bytes 1769476

commit v3 on v2

--- a/solution.py
+++ b/solution.py
@@ -35,17 +35,30 @@
     return jnp.asarray(one, BF16), jnp.asarray(two, BF16)
 
 
+def transform(fields, left, right):
+    stacked = jnp.concatenate([jnp.concatenate(pair, 0) for pair in fields], 1)
+    first = jnp.dot(left[...], stacked, preferred_element_type=F32).astype(BF16)
+    rows = [
+        jnp.concatenate([first[:N, i * N:(i + 1) * N], first[N:, i * N:(i + 1) * N]], 1)
+        for i in range(len(fields))
+    ]
+    second = jnp.dot(jnp.concatenate(rows, 0), right[...], preferred_element_type=F32)
+    return [second[i * N:(i + 1) * N] for i in range(len(fields))]
+
+
 def kernel(
     obj_hbm, probe_hbm, mw_ref, meas_hbm, corner_ref, counts_ref, widx_ref, one_hbm, two_hbm,
     obj_out, gobj, probe_out, gprobe,
-    objs, probes, meas, one, two,
+    meas, one, two,
     frame, ob, h_right, h_below, h_diag,
     patches, psi, inten, ipart_s, ipart_r, terms, pgrad, zall,
     g_send, g_recv, g_own, margin, m_right, m_below, m_diag,
     rs_send, rs_recv, ag_mine,
-    s_in, s_out, s_halo, r_halo, s_fwd, r_fwd, s_int, r_int, s_g, r_g, s_m, r_m,
+    s_in, s_halo, r_halo, s_fwd, r_fwd, s_int, r_int, s_g, r_g, s_m, r_m,
     s_rs, r_rs, s_ag, r_ag, s_share, r_share, stage_y, stage_z,
 ):
+    objs = obj_out.at[0]
+    probes = probe_out
     t = lax.axis_index("tile")
     k = lax.axis_index("mode")
     other = 1 - k
@@ -109,7 +122,7 @@
         remote(dst, dst, s_fwd.at[i], r_fwd.at[i], t, other)
         for i, (src, dst, to) in enumerate(halo_chunks())
     ]
-    halo_order = (0, 2, 1, 3, 4, 5, 6)
+    halo_order = (5, 6, 2, 3, 4, 0, 1)
 
     def margin_chunks():
         for j in range(2):
@@ -178,7 +191,7 @@
         def intensity_copy(s):
             return remote(ipart_s.at[s], ipart_r.at[s], s_int.at[s], r_int.at[s], t, other)
 
-        def forward_slot(s, _):
+        def forward_slot(s):
             row = corner_ref[0, s]
             col = corner_ref[1, s]
             q = lax.div(col, L)
@@ -194,17 +207,15 @@
                     )
             o_re = patches[s, 0]
             o_im = patches[s, 1]
-            total = None
+            fields = []
             for m in range(MODES):
                 p_re = probes[m, 0]
                 p_im = probes[m, 1]
                 e_re = (p_re * o_re - p_im * o_im).astype(BF16)
                 e_im = (p_re * o_im + p_im * o_re).astype(BF16)
-                first = jnp.dot(
-                    one[...], jnp.concatenate([e_re, e_im], 0), preferred_element_type=F32
-                ).astype(BF16)
-                first = jnp.concatenate([first[:N], first[N:]], 1)
-                wave = jnp.dot(first, two[...], preferred_element_type=F32)
+                fields.append((e_re, e_im))
+            total = None
+            for m, wave in enumerate(transform(fields, one, two)):
                 psi[s, m] = wave
                 w = mw_ref[m, widx_ref[s]]
                 part = w * (wave[:, :N] * wave[:, :N] + wave[:, N:] * wave[:, N:])
@@ -212,9 +223,13 @@
             inten[s] = total
             ipart_s[s] = total.astype(BF16)
             intensity_copy(s).start()
-            return 0
-
-        lax.fori_loop(0, SLOTS, forward_slot, 0)
+
+        def forward_pair(i, _):
+            forward_slot(2 * i)
+            forward_slot(2 * i + 1)
+            return 0
+
+        lax.fori_loop(0, SLOTS // 2, forward_pair, 0)
 
         def scatter_copy(m, p):
             peer = lax.rem(t + p, TILES)
@@ -232,46 +247,48 @@
         for m in range(MODES):
             pgrad[...] = jnp.zeros_like(pgrad)
 
-            def backward_slot(s, _):
-                w = mw_ref[m, widx_ref[s]]
-                if m == 0:
-                    intensity_copy(s).wait()
-                    live = jnp.where(s < counts_ref[0], 1.0, 0.0).astype(F32)
-                    inten[s] = (inten[s] + ipart_r[s].astype(F32) - meas[s]) * live
-                factor = w * inten[s]
-                s_re = (factor * psi[s, m, :, 0:N]).astype(BF16)
-                s_im = (factor * psi[s, m, :, N:2 * N]).astype(BF16)
-                first = jnp.dot(
-                    two[...], jnp.concatenate([s_re, s_im], 0), preferred_element_type=F32
-                ).astype(BF16)
-                first = jnp.concatenate([first[:N], first[N:]], 1)
-                chi = jnp.dot(first, one[...], preferred_element_type=F32)
-                c_re = chi[:, :N]
-                c_im = chi[:, N:]
+            def backward_pair(i):
+                fields = []
+                for s in (2 * i, 2 * i + 1):
+                    w = mw_ref[m, widx_ref[s]]
+                    if m == 0:
+                        intensity_copy(s).wait()
+                        live = jnp.where(s < counts_ref[0], 1.0, 0.0).astype(F32)
+                        inten[s] = (inten[s] + ipart_r[s].astype(F32) - meas[s]) * live
+                    factor = w * inten[s]
+                    s_re = (factor * psi[s, m, :, 0:N]).astype(BF16)
+                    s_im = (factor * psi[s, m, :, N:2 * N]).astype(BF16)
+                    fields.append((s_re, s_im))
                 p_re = probes[m, 0]
                 p_im = probes[m, 1]
-                o_re = patches[s, 0]
-                o_im = patches[s, 1]
-                t_re = p_re * c_re + p_im * c_im
-                t_im = p_re * c_im - p_im * c_re
-                if m == 0:
-                    terms[s, 0] = t_re
-                    terms[s, 1] = t_im
-                else:
-                    terms[s, 0] = terms[s, 0] + t_re
-                    terms[s, 1] = terms[s, 1] + t_im
-                pgrad[0] = pgrad[0] + o_re * c_re + o_im * c_im
-                pgrad[1] = pgrad[1] + o_re * c_im - o_im * c_re
+                for s, chi in zip((2 * i, 2 * i + 1), transform(fields, two, one)):
+                    c_re = chi[:, :N]
+                    c_im = chi[:, N:]
+                    o_re = patches[s, 0]
+                    o_im = patches[s, 1]
+                    t_re = p_re * c_re + p_im * c_im
+                    t_im = p_re * c_im - p_im * c_re
+                    if m == 0:
+                        terms[s, 0] = t_re
+                        terms[s, 1] = t_im
+                    else:
+                        terms[s, 0] = terms[s, 0] + t_re
+                        terms[s, 1] = terms[s, 1] + t_im
+                    pgrad[0] = pgrad[0] + o_re * c_re + o_im * c_im
+                    pgrad[1] = pgrad[1] + o_re * c_im - o_im * c_re
+
+            def backward_step(i, _):
+                backward_pair(i)
                 return 0
 
-            lax.fori_loop(0, SLOTS, backward_slot, 0)
+            lax.fori_loop(0, SLOTS // 2, backward_step, 0)
             rs_send[m] = pgrad[...].astype(BF16)
 
             def scatter(p, _):
                 scatter_copy(m, p).start()
                 return 0
 
-            lax.fori_loop(1, TILES, scatter, 0)
+            lax.fori_loop(1, TILES, scatter, 0, unroll=9)
 
         def spread(s, _):
             rem = lax.rem(corner_ref[1, s], L)
@@ -359,7 +376,7 @@
                 gather_copy(m, p).start()
                 return 0
 
-            lax.fori_loop(1, TILES, one_copy, 0)
+            lax.fori_loop(1, TILES, one_copy, 0, unroll=9)
 
         for m in range(MODES):
             gather(m)
@@ -398,14 +415,10 @@
         def _():
             probes[...] = probes[...] - STEP_PROBE * gprobe[...].astype(F32)
             objs[other] = objs[other] - STEP_OBJECT * gobj[0, other].astype(F32)
-            pltpu.make_async_copy(objs, obj_out.at[0], s_out.at[0]).start()
-            pltpu.make_async_copy(probes, probe_out, s_out.at[1]).start()
 
         return 0
 
     lax.fori_loop(0, ITERS, sweep, 0)
-    pltpu.make_async_copy(objs, obj_out.at[0], s_out.at[0]).wait()
-    pltpu.make_async_copy(probes, probe_out, s_out.at[1]).wait()
 
 
 def body(obj, probe, mode_weights, measured, corner, counts, weight_index):
@@ -418,16 +431,14 @@
         kernel,
         name="ptycho",
         out_shape=(
-            jax.ShapeDtypeStruct(obj.shape, F32),
-            jax.ShapeDtypeStruct(obj.shape, BF16),
-            jax.ShapeDtypeStruct(probe.shape, F32),
-            jax.ShapeDtypeStruct(probe.shape, BF16),
+            pltpu.VMEM(obj.shape, F32),
+            pltpu.VMEM(obj.shape, BF16),
+            pltpu.VMEM(probe.shape, F32),
+            pltpu.VMEM(probe.shape, BF16),
         ),
         in_specs=[hbm, hbm, smem, hbm, smem, smem, smem, hbm, hbm],
-        out_specs=(hbm, vmem, hbm, vmem),
+        out_specs=(vmem, vmem, vmem, vmem),
         scratch_shapes=[
-            pltpu.VMEM((2, TILE, TILE), F32),
-            pltpu.VMEM((MODES, 2, N, N), F32),
             pltpu.VMEM((SLOTS, N, N), F32),
             pltpu.VMEM((2 * N, 2 * N), BF16),
             pltpu.VMEM((2 * N, 2 * N), BF16),
@@ -454,12 +465,12 @@
             pltpu.VMEM((MODES, 2, N, N), BF16),
             pltpu.VMEM((MODES, 1024, L), BF16),
             pltpu.VMEM((MODES, 16, L), BF16),
-            dma((5,)), dma((2,)), dma((7,)), dma((7,)), dma((7,)), dma((7,)), dma((4,)), dma((4,)),
+            dma((5,)), dma((7,)), dma((7,)), dma((7,)), dma((7,)), dma((4,)), dma((4,)),
             dma((2,)), dma((2,)), dma((7,)), dma((7,)),
             dma((2,)), dma((2,)), dma((2,)), dma((2,)), dma, dma, regular, regular,
         ],
         compiler_params=pltpu.CompilerParams(
-            collective_id=0, has_side_effects=True, vmem_limit_bytes=60 << 20
+            collective_id=0, has_side_effects=True, vmem_limit_bytes=54 << 20
         ),
     )(obj, probe, mode_weights.T, measured, corner.T, counts, weight_index, *dft_tables())
     return (

time: 118 us -> 104 us (0.88)
  Pallas kernels: 113 us -> 99.9 us
  other arithmetic: 3.74 us -> 2.24 us
    pallas_call x1, Pallas kernels: 113 us -> 99.9 us  [body(): pl.pallas_call(kernel, name='ptycho', out_shape=(pltpu.VMEM(obj.shape, F3...]
    sub x1, other arithmetic: 2.59 us -> 1.09 us  [body(): probe_1 - STEP_PROBE * grad_probe.astype(F32)]
where the time goes in v3:
time: 104 us; the launch traced here: 103 us
  Pallas kernels  99.9 us (96%)
  other arithmetic  2.24 us (2%)
  between operations  1.29 us (1%)
    pallas_call x1, Pallas kernels, body(): pl.pallas_call(kernel, name='ptycho', out_shape=(pltpu.VMEM(obj.shape, F3...  99.9 us

profile of v3, /device:TPU:1, one launch (start us, length us, event | category | flops | bytes accessed | tf_op | source)
XLA Modules:
  0.0 103.5 jit_solution(13727908105820887895)
XLA Ops:
  1.3 99.9 %ptycho.1 = (f32[1,2,384,384]{3,2,1,0:T(8,128)S(1)}, bf16[1,2,384,384]{3,2,1,0:T(8,128)(2,1)S(1)}, f32[2,2,256,256]{3,2,1,0:T(8,128)S(1)}, bf16[2,2,256,256]{3,2,1,0:T(8,128)(2,1)S(1)}) custom-call(f32[1,2,384,384]{3,2,1,0:T(8,128)} %obj_hbm.1, f32[2,2,256,256]{3,2,1,0:T(8,128)} %probe_hbm.1, f32[2,8]{1,0:T(2,128)} %bitcast.2, f32[4,256,256]{2,1,0:T(8,128)} %meas_hbm.1, ...), custom_call_target="tpu_custom_call" | custom-call | tf_op jit(solution)/shard_map/ptycho/pallas_call | solution.py:430
  101.2 1.1 %multiply_subtract_fusion.1 = f32[2,2,256,256]{3,2,1,0:T(8,128)} fusion(f32[2,2,256,256]{3,2,1,0:T(8,128)S(1)} %get-tuple-element.8, bf16[2,2,256,256]{3,2,1,0:T(8,128)(2,1)S(1)} %get-tuple-element.9), kind=kLoop, calls=%fused_computation.1 | loop fusion | flops 786432 | bytes 2621440 | tf_op jit(solution)/shard_map/sub | solution.py:478
  102.3 1.1 %multiply_subtract_fusion = f32[1,2,384,384]{3,2,1,0:T(8,128)} fusion(f32[1,2,384,384]{3,2,1,0:T(8,128)S(1)} %get-tuple-element.6, bf16[1,2,384,384]{3,2,1,0:T(8,128)(2,1)S(1)} %get-tuple-element.7), kind=kLoop, calls=%fused_computation | loop fusion | flops 884736 | bytes 2949120 | tf_op jit(solution)/shard_map/sub | solution.py:477

commit v4 on v3

--- a/solution.py
+++ b/solution.py
@@ -381,11 +381,12 @@
         for m in range(MODES):
             gather(m)
 
-        for send in margin_sends:
-            send.wait()
         more = it < ITERS - 1
+        share = remote(gobj.at[0, k], gobj.at[0, k], s_share, r_share, t, other)
         for j in range(3):
             cols = slice(j * L, (j + 1) * L)
+            for i in ((0, 2, 5), (1, 3, 6), (4,))[j]:
+                margin_sends[i].wait()
             upper = g_own[j, 0:N] + m_below[j].astype(F32)
             lower = g_own[j, N:TILE]
             if j < 2:
@@ -393,18 +394,16 @@
                 lower = lower + m_right[j, N:TILE].astype(F32)
             gobj[0, k, 0:N, cols] = upper.astype(BF16)
             gobj[0, k, N:TILE, cols] = lower.astype(BF16)
-        share = remote(gobj.at[0, k], gobj.at[0, k], s_share, r_share, t, other)
-        share.start()
-
-        @pl.when(more)
-        def _():
-            for j in range(3):
-                cols = slice(j * L, (j + 1) * L)
+
+            @pl.when(more)
+            def _():
                 now = objs[k, :, cols] - STEP_OBJECT * gobj[0, k, :, cols].astype(F32)
                 objs[k, :, cols] = now
                 ob[j] = now.astype(BF16)
-            for i in halo_order:
-                halo_sends[i].start()
+                for i in ((5, 2, 0), (6, 3, 1), (4,))[j]:
+                    halo_sends[i].start()
+
+        share.start()
 
         for m in range(MODES):
             whole = rs_recv.at[m, pl.ds(16, 63 * 16)]

time: 104 us -> 103 us (level)
  no operation moved by 1% of the time
where the time goes in v4:
time: 103 us
  Pallas kernels  99 us (96%)
  other arithmetic  2.24 us (2%)
  between operations  1.29 us (1%)
    pallas_call x1, Pallas kernels, body(): pl.pallas_call(kernel, name='ptycho', out_shape=(pltpu.VMEM(obj.shape, F3...  99 us

profile of v4, /device:TPU:1, one launch (start us, length us, event | category | flops | bytes accessed | tf_op | source)
XLA Modules:
  0.0 102.5 jit_solution(12669885535821038281)
XLA Ops:
  1.3 99.0 %ptycho.1 = (f32[1,2,384,384]{3,2,1,0:T(8,128)S(1)}, bf16[1,2,384,384]{3,2,1,0:T(8,128)(2,1)S(1)}, f32[2,2,256,256]{3,2,1,0:T(8,128)S(1)}, bf16[2,2,256,256]{3,2,1,0:T(8,128)(2,1)S(1)}) custom-call(f32[1,2,384,384]{3,2,1,0:T(8,128)} %obj_hbm.1, f32[2,2,256,256]{3,2,1,0:T(8,128)} %probe_hbm.1, f32[2,8]{1,0:T(2,128)} %bitcast.2, f32[4,256,256]{2,1,0:T(8,128)} %meas_hbm.1, ...), custom_call_target="tpu_custom_call" | custom-call | tf_op jit(solution)/shard_map/ptycho/pallas_call | solution.py:429
  100.3 1.1 %multiply_subtract_fusion.1 = f32[2,2,256,256]{3,2,1,0:T(8,128)} fusion(f32[2,2,256,256]{3,2,1,0:T(8,128)S(1)} %get-tuple-element.8, bf16[2,2,256,256]{3,2,1,0:T(8,128)(2,1)S(1)} %get-tuple-element.9), kind=kLoop, calls=%fused_computation.1 | loop fusion | flops 786432 | bytes 2621440 | tf_op jit(solution)/shard_map/sub | solution.py:477
  101.4 1.1 %multiply_subtract_fusion = f32[1,2,384,384]{3,2,1,0:T(8,128)} fusion(f32[1,2,384,384]{3,2,1,0:T(8,128)S(1)} %get-tuple-element.6, bf16[1,2,384,384]{3,2,1,0:T(8,128)(2,1)S(1)} %get-tuple-element.7), kind=kLoop, calls=%fused_computation | loop fusion | flops 884736 | bytes 2949120 | tf_op jit(solution)/shard_map/sub | solution.py:476

commit v5 on v4

--- a/solution.py
+++ b/solution.py
@@ -232,14 +232,14 @@
         lax.fori_loop(0, SLOTS // 2, forward_pair, 0)
 
         def scatter_copy(m, p):
-            peer = lax.rem(t + p, TILES)
+            peer = lax.rem(t + 21 * p, TILES)
             return remote(
                 shard(rs_send, m, peer), rs_recv.at[m, pl.ds(p * 16, 16)],
                 s_rs.at[m], r_rs.at[m], peer, k,
             )
 
         def gather_copy(m, p):
-            peer = lax.rem(t + p, TILES)
+            peer = lax.rem(t + 21 * p, TILES)
             return remote(
                 ag_mine.at[m], shard(gprobe, m, t), s_ag.at[m], r_ag.at[m], peer, k
             )

time: 103 us -> 104 us (level)
  no operation moved by 1% of the time
where the time goes in v5:
time: 104 us; the launch traced here: 103 us
  Pallas kernels  99.1 us (95%)
  other arithmetic  2.24 us (2%)
  between operations  1.29 us (1%)
    pallas_call x1, Pallas kernels, body(): pl.pallas_call(kernel, name='ptycho', out_shape=(pltpu.VMEM(obj.shape, F3...  99.1 us

profile of v5, /device:TPU:1, one launch (start us, length us, event | category | flops | bytes accessed | tf_op | source)
XLA Modules:
  0.0 102.6 jit_solution(14235085479890032462)
XLA Ops:
  1.3 99.1 %ptycho.1 = (f32[1,2,384,384]{3,2,1,0:T(8,128)S(1)}, bf16[1,2,384,384]{3,2,1,0:T(8,128)(2,1)S(1)}, f32[2,2,256,256]{3,2,1,0:T(8,128)S(1)}, bf16[2,2,256,256]{3,2,1,0:T(8,128)(2,1)S(1)}) custom-call(f32[1,2,384,384]{3,2,1,0:T(8,128)} %obj_hbm.1, f32[2,2,256,256]{3,2,1,0:T(8,128)} %probe_hbm.1, f32[2,8]{1,0:T(2,128)} %bitcast.2, f32[4,256,256]{2,1,0:T(8,128)} %meas_hbm.1, ...), custom_call_target="tpu_custom_call" | custom-call | tf_op jit(solution)/shard_map/ptycho/pallas_call | solution.py:429
  100.4 1.1 %multiply_subtract_fusion.1 = f32[2,2,256,256]{3,2,1,0:T(8,128)} fusion(f32[2,2,256,256]{3,2,1,0:T(8,128)S(1)} %get-tuple-element.8, bf16[2,2,256,256]{3,2,1,0:T(8,128)(2,1)S(1)} %get-tuple-element.9), kind=kLoop, calls=%fused_computation.1 | loop fusion | flops 786432 | bytes 2621440 | tf_op jit(solution)/shard_map/sub | solution.py:477
  101.5 1.1 %multiply_subtract_fusion = f32[1,2,384,384]{3,2,1,0:T(8,128)} fusion(f32[1,2,384,384]{3,2,1,0:T(8,128)S(1)} %get-tuple-element.6, bf16[1,2,384,384]{3,2,1,0:T(8,128)(2,1)S(1)} %get-tuple-element.7), kind=kLoop, calls=%fused_computation | loop fusion | flops 884736 | bytes 2949120 | tf_op jit(solution)/shard_map/sub | solution.py:476
